TPU v7x, 32 devices: a whole 2x2x4 slice. The times are simulated.
32 devices in a mesh: lat: 4 (over x, core), dp: 8 (over z, y).
Axes of the slice: x: 2, y: 2, z: 4, core: 2. Of those that a mesh axis runs over, the one named last changes fastest.
Arguments:
- inputs: bfloat16 [8, 4, 128, 384], P('dp', 'lat'), may hold values from -6 to 6
- cotangent: bfloat16 [8, 4, 128, 384], P('dp', 'lat'), may hold values from -6 to 6
- kernel_tiles: bfloat16 [4, 6, 3, 128, 128], P('lat'), may hold values from -0.21875 to 0.21875
- mix_weight: bfloat16 [1152, 384], replicated, may hold values from -0.1875 to 0.1875
- slot_row: int32 [4, 6], P('lat'), may hold values from -1 to 1, as said below
- slot_lon: int32 [4, 6], P('lat'), may hold values from -1 to 1
- slot_count: int32 [4], P('lat'), may hold values from 3 to 6, as said below
- scale_exps: int32 [1152, 3], P('dp'), may hold values from -1 to 1
Outputs:
- block_out: bfloat16 [8, 4, 128, 384], P('dp', 'lat')
- input_grad: bfloat16 [8, 4, 128, 384], P('dp', 'lat')
- weight_grad: float32 [1152, 384], P('dp')
Inputs may be any that keep to these rules, and one draw needn't show every extreme that they name: `slot_row`: slot 0 of every row has offset 0, slot 1 offset -1 and slot 2 offset +1. `slot_count`: 6 at the first and the last row; fewer at the other rows.
All inputs are finite; a program needn't handle non-finite values.
Results may differ from a plain program's by a relative error of at most 0.0095.
Values may be sent and summed in bfloat16 or wider, within the bound.
A program may use at most 64 MiB of HBM per device.

v0:
```python
import math

import jax
import jax.numpy as jnp
from jax import lax
from jax.sharding import PartitionSpec as P


def extended_2(cells, sides, width):
    for axis, dim in sides:
        count = lax.axis_size(axis)
        ends = count - 1
        head = lax.slice_in_dim(cells, 0, width, axis=dim)
        tail = lax.slice_in_dim(cells, cells.shape[dim] - width, cells.shape[dim], axis=dim)
        cells = jnp.concatenate(
            [
                lax.ppermute(tail, axis, [(i, (i + 1) % count) for i in range(ends)]),
                cells,
                lax.ppermute(head, axis, [((i + 1) % count, i) for i in range(ends)]),
            ],
            axis=dim,
        )
    return cells


def local(inputs, cotangent, kernel_tiles, mix_weight, slot_row, slot_lon, slot_count, scale_exps):
    rows_here = inputs.shape[1]
    lon_width = inputs.shape[2]
    channels = inputs.shape[3]
    slot_total = kernel_tiles.shape[1]
    basis_count = kernel_tiles.shape[2]
    tile_size = kernel_tiles.shape[3]
    lon_blocks = lon_width // tile_size
    points = rows_here * lon_width
    mix_major = (
        mix_weight.reshape(channels, basis_count, channels)
        .transpose(1, 0, 2)
        .reshape(basis_count * channels, channels)
    )
    extended = extended_2(inputs, (("lat", 1),), 1)
    blocks = extended[0].reshape(rows_here + 2, lon_blocks, tile_size, channels)
    row_ids = jnp.arange(rows_here, dtype=jnp.int32)
    blk_ids = jnp.arange(lon_blocks, dtype=jnp.int32)
    sources = []
    shifts = []
    masked = []
    for slot_index in range(slot_total):
        sources.append(row_ids + slot_row[:, slot_index] + 1)
        shifts.append((blk_ids[None, :] + slot_lon[:, slot_index][:, None]) % lon_blocks)
        keep_mask = (slot_index < slot_count).astype(jnp.bfloat16)
        masked.append(kernel_tiles[:, slot_index] * keep_mask[:, None, None, None])
    accum = jnp.zeros((rows_here, lon_blocks, tile_size, basis_count, channels), jnp.float32)
    for slot_index in range(slot_total):
        picked = blocks[sources[slot_index][:, None], shifts[slot_index]]
        accum = accum + jnp.einsum(
            "rkpq,rjqc->rjpkc", masked[slot_index], picked, preferred_element_type=jnp.float32
        )
    basis_out = accum.reshape(points, basis_count * channels).astype(jnp.bfloat16)
    mixed = jnp.dot(basis_out, mix_major, preferred_element_type=jnp.float32)
    gate_value = jax.nn.sigmoid(mixed)
    flat_in = inputs.reshape(points, channels).astype(jnp.float32)
    result = (flat_in + mixed * gate_value).astype(jnp.bfloat16).reshape(inputs.shape)
    flat_cot = cotangent.reshape(points, channels).astype(jnp.float32)
    dmixed = (flat_cot * gate_value * (1.0 + mixed * (1.0 - gate_value))).astype(jnp.bfloat16)
    dbasis = lax.dot_general(
        dmixed, mix_major, (((1,), (1,)), ((), ())), preferred_element_type=jnp.float32
    ).astype(jnp.bfloat16)
    dbasis = dbasis.reshape(rows_here, lon_blocks, tile_size, basis_count, channels)
    back_ext = jnp.zeros((rows_here + 2, lon_blocks, tile_size, channels), jnp.float32)
    for slot_index in range(slot_total):
        slot_term = jnp.einsum(
            "rkpq,rjpkc->rjqc", masked[slot_index], dbasis, preferred_element_type=jnp.float32
        )
        back_ext = back_ext.at[sources[slot_index][:, None], shifts[slot_index]].add(slot_term)
    rim_rows = jnp.concatenate([back_ext[:1], back_ext[rows_here + 1 :]], axis=0).reshape(
        2, lon_width, channels
    )
    returned = extended_2(rim_rows.astype(jnp.bfloat16), (("lat", 0),), 1).astype(rim_rows.dtype)
    inner_grad = back_ext[1 : rows_here + 1].reshape(rows_here, lon_width, channels)
    inner_grad = inner_grad.at[0].add(returned[0])
    inner_grad = inner_grad.at[rows_here - 1].add(returned[3])
    grad_in = (cotangent[0].astype(jnp.float32) + inner_grad).astype(jnp.bfloat16)[None]
    major_part = lax.dot_general(
        basis_out, dmixed, (((0,), (0,)), ((), ())), preferred_element_type=jnp.float32
    )
    partial_value = (
        major_part.reshape(basis_count, channels, channels)
        .transpose(1, 0, 2)
        .reshape(channels * basis_count, channels)
    )
    row_part = lax.psum_scatter(partial_value, "dp", scatter_dimension=0, tiled=True)
    grad_total = lax.psum(row_part, "lat")
    factor = jnp.repeat(jnp.exp2(-scale_exps.astype(jnp.float32)), tile_size, axis=1)
    count_all = lax.axis_size("dp") * inputs.shape[0] * lax.axis_size("lat") * rows_here * lon_width
    weight_grad = grad_total * factor / math.sqrt(count_all)
    return (result, grad_in, weight_grad)


def solution(mesh):
    in_specs = (
        P("dp", "lat", None, None),
        P("dp", "lat", None, None),
        P("lat", None, None, None, None),
        P(),
        P("lat", None),
        P("lat", None),
        P("lat"),
        P("dp", None),
    )
    out_specs = (P("dp", "lat", None, None), P("dp", "lat", None, None), P("dp", None))
    return jax.shard_map(local, mesh=mesh, in_specs=in_specs, out_specs=out_specs, check_vma=False)
```

profile of v0, /device:TPU:0, one launch (start us, length us, event | category | flops | bytes accessed | tf_op | source)
XLA Modules:
  0.0 143.1 jit_solution(14742324878770142051)
XLA Ops:
  7.2 2.4 %collective-permute-start = (bf16[1,1,128,384]{3,2,1,0:T(8,128)(2,1)}, bf16[1,1,128,384]{3,2,1,0:T(8,128)(2,1)S(1)}, u32[]{:S(2)}, u32[]{:S(2)}) collective-permute-start(bf16[1,1,128,384]{3,2,1,0:T(8,128)(2,1)} %param.24), channel_id=1, source_target_pairs={{0,8},{8,16},{16,24},{1,9},{9,17},{17,25},{2,10},{10,18},{18,26},{... | collective-permute-start | bytes 294920 | tf_op jit(solution)/shard_map/ppermute | solution.py:17
  9.6 1.3 collective-permute-start.1
  10.9 1.5 %fusion.90 = (s32[1,1]{1,0:T(1,128)}, s32[1,1]{1,0:T(1,128)}, s32[1,1]{1,0:T(1,128)}, s32[1,1]{1,0:T(1,128)}, s32[1,1]{1,0:T(1,128)}, /*index=5*/s32[1,1]{1,0:T(1,128)}) fusion(s32[1,6]{1,0:T(1,128)} %param.28), kind=kLoop, calls=%fused_computation.149 | loop fusion | bytes 48 | tf_op jit(solution)/shard_map/slice | solution.py:48
  20.8 2.3 %reshape.563 = bf16[384,3,384]{2,1,0:T(4,128)(2,1)S(1)} reshape(bf16[1152,384]{1,0:T(8,128)(2,1)} %param.27) | data formatting | bytes 1769472 | tf_op jit(solution)/shard_map/reshape | solution.py:36
  23.5 0.6 copy-done
  24.4 0.3 fusion.35
  24.7 0.3 fusion.37
  25.1 0.3 fusion.39
  25.4 0.3 fusion.41
  25.7 0.3 fusion.4
  26.1 0.4 fusion.91
  26.6 0.4 convolution_bitcast_fusion
  27.0 1.2 copy.43
  28.2 2.3 %reshape.581 = f32[1152,384]{1,0:T(8,128)} reshape(f32[384,3,384]{2,1,0:T(4,128)S(1)} %copy.43) | data formatting | bytes 3538944 | tf_op jit(solution)/shard_map/reshape | solution.py:89
  30.6 0.6 copy-done.6
  31.3 0.8 and_reduce_fusion.4
  32.1 0.8 and_reduce_fusion.2
  32.9 0.7 and_reduce_fusion
  33.6 0.4 convolution_convert_fusion
  34.3 0.9 fusion.7
  35.2 0.9 fusion.10
  36.1 1.0 fusion.13
  37.1 0.9 fusion.16
  38.1 0.8 fusion.19
  38.9 0.9 fusion.22
  39.9 1.3 collective-permute-start.3
  41.2 5.8 %collective-permute-start.2 = (bf16[1,128,384]{2,1,0:T(8,128)(2,1)S(1)}, bf16[1,128,384]{2,1,0:T(8,128)(2,1)S(1)}, u32[]{:S(2)}, u32[]{:S(2)}) collective-permute-start(bf16[1,128,384]{2,1,0:T(8,128)(2,1)S(1)} %get-tuple-element.171), channel_id=1, source_target_pairs={{0,8},{8,16},{16,24},{1,9},{9,17},{17,25},{2,10},{10,18},{18,26},{... | collective-permute-start | bytes 294920 | tf_op jit(solution)/shard_map/ppermute | solution.py:17
  47.0 0.7 fusion.63
  47.7 53.7 %reduce-scatter.2.cloned.1.call-done = f32[144,384]{1,0:T(8,128)} async-done(((f32[1152,384]{1,0:T(8,128)}), f32[144,384]{1,0:T(8,128)}) %reduce-scatter.2.cloned.1.call-update) | async-done | bytes 221200 | tf_op jit(solution)/shard_map/reduce_scatter | solution.py:91
  101.4 0.7 fusion.32
  102.1 32.3 %all-reduce.2.cloned.1.call-done = f32[144,384]{1,0:T(8,128)} async-done(((f32[144,384]{1,0:T(8,128)}), f32[144,384]{1,0:T(8,128)}) %all-reduce.2.cloned.1.call-update) | async-done | bytes 221200 | tf_op jit(solution)/shard_map/psum | solution.py:92
  134.6 1.7 %fusion.24 = f32[144,384]{1,0:T(8,128)} fusion(f32[144,384]{1,0:T(8,128)} %all-reduce.2.cloned.1.call-done, f32[18,8,3,128]{3,2,1,0:T(4,128)S(1)} %bitcast.272), kind=kLoop, calls=%fused_computation.36 | loop fusion | flops 110592 | bytes 663552 | tf_op jit(solution)/shard_map/div | solution.py:95
  (36 shorter events, 1.7 us)
Async XLA Ops:
  7.2 94.2 %reduce-scatter.2.cloned.1.call-start = ((), (), s32[]{:S(2)}) async-start(), calls=%async_computation.1 | async-start | bytes 1990656 | tf_op jit(solution)/shard_map/reduce_scatter | solution.py:91
  7.2 16.2 %collective-permute-start = (bf16[1,1,128,384]{3,2,1,0:T(8,128)(2,1)}, bf16[1,1,128,384]{3,2,1,0:T(8,128)(2,1)S(1)}, u32[]{:S(2)}, u32[]{:S(2)}) collective-permute-start(bf16[1,1,128,384]{3,2,1,0:T(8,128)(2,1)} %param.24), channel_id=1, source_target_pairs={{0,8},{8,16},{16,24},{1,9},{9,17},{17,25},{2,10},{10,18},{18,26},{... | collective-permute-start | bytes 294920 | tf_op jit(solution)/shard_map/ppermute | solution.py:17
  9.6 13.9 %collective-permute-start.1 = (bf16[1,1,128,384]{3,2,1,0:T(8,128)(2,1)}, bf16[1,1,128,384]{3,2,1,0:T(8,128)(2,1)S(1)}, u32[]{:S(2)}, u32[]{:S(2)}) collective-permute-start(bf16[1,1,128,384]{3,2,1,0:T(8,128)(2,1)} %param.24), channel_id=1, source_target_pairs={{8,0},{16,8},{24,16},{9,1},{17,9},{25,17},{10,2},{18,10},{26,18},{... | collective-permute-start | bytes 294920 | tf_op jit(solution)/shard_map/ppermute | solution.py:19
  20.8 2.7 %copy-start.3 = (bf16[1,1,128,384]{3,2,1,0:T(8,128)(2,1)S(1)}, bf16[1,1,128,384]{3,2,1,0:T(8,128)(2,1)}, u32[]{:S(2)}) copy-start(bf16[1,1,128,384]{3,2,1,0:T(8,128)(2,1)} %param.24) | copy-start | bytes 294916
  23.0 1.1 copy-start
  25.7 0.9 copy-start.2
  30.5 0.7 copy-start.6
  30.5 0.8 copy-start.5
  30.5 3.8 %copy-start.1 = (bf16[1,6,3,128,128]{4,3,2,1,0:T(8,128)(2,1)S(1)}, bf16[1,6,3,128,128]{4,3,2,1,0:T(8,128)(2,1)}, u32[]{:S(2)}) copy-start(bf16[1,6,3,128,128]{4,3,2,1,0:T(8,128)(2,1)} %param.26) | copy-start | bytes 1769476
  30.6 103.8 %all-reduce.2.cloned.1.call-start = ((), (), s32[]{:S(2)}) async-start(), calls=%async_computation.2 | async-start | bytes 442368 | tf_op jit(solution)/shard_map/psum | solution.py:92
  37.1 9.9 %copy-start.4 = (bf16[1,1,128,384]{3,2,1,0:T(8,128)(2,1)S(1)}, bf16[1,1,128,384]{3,2,1,0:T(8,128)(2,1)}, u32[]{:S(2)}) copy-start(bf16[1,1,128,384]{3,2,1,0:T(8,128)(2,1)} %param.24) | copy-start | bytes 294916
  39.9 61.5 %collective-permute-start.3 = (bf16[1,128,384]{2,1,0:T(8,128)(2,1)S(1)}, bf16[1,128,384]{2,1,0:T(8,128)(2,1)S(1)}, u32[]{:S(2)}, u32[]{:S(2)}) collective-permute-start(bf16[1,128,384]{2,1,0:T(8,128)(2,1)S(1)} %get-tuple-element.172), channel_id=1, source_target_pairs={{8,0},{16,8},{24,16},{9,1},{17,9},{25,17},{10,2},{18,10},{26,18},{... | collective-permute-start | bytes 294920 | tf_op jit(solution)/shard_map/ppermute | solution.py:19
  41.2 60.2 %collective-permute-start.2 = (bf16[1,128,384]{2,1,0:T(8,128)(2,1)S(1)}, bf16[1,128,384]{2,1,0:T(8,128)(2,1)S(1)}, u32[]{:S(2)}, u32[]{:S(2)}) collective-permute-start(bf16[1,128,384]{2,1,0:T(8,128)(2,1)S(1)} %get-tuple-element.171), channel_id=1, source_target_pairs={{0,8},{8,16},{16,24},{1,9},{9,17},{17,25},{2,10},{10,18},{18,26},{... | collective-permute-start | bytes 294920 | tf_op jit(solution)/shard_map/ppermute | solution.py:17
Sparse Core Ops, SparseCore 0:
  30.7 70.6 reduce-scatter.1
  103.8 30.4 all-reduce.1
where the time goes:
time: 144 us; the launch traced here: 143 us
  waiting for transfers between devices  86 us (60%)
  between operations  22.7 us (16%)
  starting transfers between devices  10.8 us (8%)
  local copies, waits for them, and re-layouts  9.43 us (7%)
  matrix products  8.56 us (6%)
  other arithmetic  5.63 us (4%)
    reduce_scatter x1, waiting for transfers between devices, local(): lax.psum_scatter(partial_value, 'dp', scatter_dimension=0, tiled=True)  53.7 us
    psum x1, waiting for transfers between devices, local(): grad_total = lax.psum(row_part, 'lat')  32.3 us
    ppermute x2, starting transfers between devices, extended_2(): lax.ppermute(tail, axis, [(i, (i + 1) % count) for i in range(ends)])  8.13 us
    dot_general x6, matrix products, local(): jnp.einsum('rkpq,rjpkc->rjqc', masked[slot_index], dbasis, preferred_elem...  5.43 us
  transfers between devices with their start and end apart: 6, of which 2 were waited for; matrix products, arithmetic and copies ran while one was open for 10% of the time, Pallas kernels for 0%

commit v1 on v0

--- a/solution.py
+++ b/solution.py
@@ -3,6 +3,8 @@
 import jax
 import jax.numpy as jnp
 from jax import lax
+from jax.experimental import pallas as pl
+from jax.experimental.pallas import tpu as pltpu
 from jax.sharding import PartitionSpec as P
 
 
@@ -96,6 +98,291 @@
     return (result, grad_in, weight_grad)
 
 
+MESH = pl.DeviceIdType.MESH
+TILE = 16
+LANES = 128
+
+
+def dot(a, b, da, db):
+    return lax.dot_general(a, b, (((da,), (db,)), ((), ())), preferred_element_type=jnp.float32)
+
+
+def fused(
+    row_ref, count_ref, scale_ref, x_hbm, cot_hbm, tiles_hbm, w_hbm,
+    out_ref, gin_ref, wg_ref,
+    xs, cot, tiles, w, wk, tmat, bas, dmix, dbas, back, rim, gt, r1, s1, r2, q, gk,
+    load_sem, halo_s, halo_r, fac_s, fac_r, xy_s, xy_r, rim_s, rim_r, z_s, z_r, lat_s, lat_r,
+):
+    lat = lax.axis_index("lat")
+    dp = lax.axis_index("dp")
+    last = 3
+    x, c = lat // 2, lat % 2
+    z, y = dp // 2, dp % 2
+    slots, basis = tiles.shape[0], tiles.shape[1]
+    size = tiles.shape[2]
+    chans = w.shape[1]
+    f32, bf16 = jnp.float32, jnp.bfloat16
+
+    loads = [
+        pltpu.make_async_copy(tiles_hbm.at[0], tiles, load_sem.at[0]),
+        pltpu.make_async_copy(w_hbm, w, load_sem.at[1]),
+        pltpu.make_async_copy(x_hbm.at[0, 0], xs.at[0], load_sem.at[2]),
+        pltpu.make_async_copy(cot_hbm.at[0, 0], cot, load_sem.at[3]),
+    ]
+    barrier = pltpu.get_barrier_semaphore()
+    x_lat = (1 - x) * 2 + c
+    c_lat = x * 2 + (1 - c)
+    xc_lat = 3 - lat
+    y_dp = z * 2 + (1 - y)
+    z_dps = [((z + o) % 4) * 2 + y for o in (1, 2, 3)]
+    friends = [(x_lat, dp), (c_lat, dp), (xc_lat, dp), (lat, y_dp), (x_lat, y_dp)]
+    friends += [(lat, d) for d in z_dps]
+    for friend in friends:
+        pl.semaphore_signal(barrier, inc=1, device_id=friend, device_id_type=MESH)
+    loads[2].start()
+    loads[0].start()
+    loads[1].start()
+    loads[3].start()
+    pl.semaphore_wait(barrier, len(friends))
+
+    def remote(src, dst, send, recv, target):
+        return pltpu.make_async_remote_copy(
+            src_ref=src, dst_ref=dst, send_sem=send, recv_sem=recv,
+            device_id=target, device_id_type=MESH,
+        )
+
+    down = remote(x_hbm.at[0, 0], xs.at[1], halo_s.at[0], halo_r.at[0], (lat + 1, dp))
+    up = remote(x_hbm.at[0, 0], xs.at[2], halo_s.at[1], halo_r.at[1], (lat - 1, dp))
+
+    @pl.when(lat < last)
+    def _():
+        down.start()
+
+    @pl.when(lat > 0)
+    def _():
+        up.start()
+
+    @pl.when(lat == 0)
+    def _():
+        xs[1] = jnp.zeros(xs.shape[1:], bf16)
+        rim[2] = jnp.zeros(rim.shape[1:], bf16)
+
+    @pl.when(lat == last)
+    def _():
+        xs[2] = jnp.zeros(xs.shape[1:], bf16)
+        rim[3] = jnp.zeros(rim.shape[1:], bf16)
+
+    gt[:, 3, :, 96:112, :] = jnp.zeros((2, 4, TILE, LANES), bf16)
+
+    loads[0].wait()
+    count = count_ref[0]
+    offs = (0, -1, 1)
+    weight = [
+        [jnp.where(jnp.logical_and(row_ref[0, s] == d, s < count), 1.0, 0.0).astype(f32) for s in range(3, slots)]
+        for d in offs
+    ]
+    for k in range(basis):
+        extra = [tiles[s, k].astype(f32) for s in range(3, slots)]
+        for n in range(3):
+            total = tiles[n, k].astype(f32)
+            for t, e in zip(weight[n], extra):
+                total = total + t * e
+            tmat[k * size : (k + 1) * size, n * size : (n + 1) * size] = total.astype(bf16)
+
+    loads[1].wait()
+    blk = 64
+    r = lax.broadcasted_iota(jnp.int32, (basis * blk, basis * blk), 0)
+    col = lax.broadcasted_iota(jnp.int32, (basis * blk, basis * blk), 1)
+    kk = (r >= blk).astype(jnp.int32) + (r >= 2 * blk).astype(jnp.int32)
+    perm = jnp.where(col == 3 * (r - blk * kk) + kk, 1.0, 0.0).astype(bf16)
+    for b in range(chans // blk):
+        part = dot(perm, w[b * basis * blk : (b + 1) * basis * blk, :], 1, 0).astype(bf16)
+        for k in range(basis):
+            wk[k, b * blk : (b + 1) * blk, :] = part[k * blk : (k + 1) * blk, :]
+
+    loads[2].wait()
+    loads[3].wait()
+
+    @pl.when(lat > 0)
+    def _():
+        down.wait_recv()
+
+    @pl.when(lat < last)
+    def _():
+        up.wait_recv()
+
+    bas[0] = dot(tmat[...], xs[...].reshape(3 * size, chans), 1, 0).astype(bf16)
+    send_bas = remote(bas.at[0], bas.at[1], fac_s.at[0], fac_r.at[0], (c_lat, dp))
+    send_bas.start()
+    mixed = dot(bas[0, 0:size, :], wk[0], 1, 0)
+    for k in range(1, basis):
+        mixed = mixed + dot(bas[0, k * size : (k + 1) * size, :], wk[k], 1, 0)
+    gate = jax.nn.sigmoid(mixed)
+    dmix[0] = (cot[...].astype(f32) * gate * (1.0 + mixed * (1.0 - gate))).astype(bf16)
+    send_dmix = remote(dmix.at[0], dmix.at[1], fac_s.at[1], fac_r.at[1], (c_lat, dp))
+    send_dmix.start()
+    out_ref[0, 0] = (xs[0].astype(f32) + mixed * gate).astype(bf16)
+
+    dm = dmix[0]
+    for k in range(basis):
+        dbas[k * size : (k + 1) * size, :] = dot(dm, wk[k], 1, 1).astype(bf16)
+
+    send_bas.wait_recv()
+    send_dmix.wait_recv()
+    both = dmix[...].reshape(2 * size, chans)
+    for k in range(basis):
+        lhs = jnp.concatenate([bas[0, k * size : (k + 1) * size, :], bas[1, k * size : (k + 1) * size, :]], axis=0)
+        grad = dot(lhs, both, 0, 0).astype(bf16)
+        for d in range(8):
+            for i in range(3):
+                for j in range(3):
+                    part, at = divmod((k * 3 + i) * 3 + j, 7)
+                    lo = 48 * d + TILE * i
+                    gt[d % 2, part, d // 2, at * TILE : (at + 1) * TILE, :] = grad[
+                        lo : lo + TILE, j * LANES : (j + 1) * LANES
+                    ]
+
+    xy = [
+        remote(gt.at[1 - y, x_lat], r1.at[2], xy_s.at[2], xy_r.at[2], (x_lat, y_dp)),
+        remote(gt.at[y, x_lat], r1.at[0], xy_s.at[0], xy_r.at[0], (x_lat, dp)),
+        remote(gt.at[1 - y, lat], r1.at[1], xy_s.at[1], xy_r.at[1], (lat, y_dp)),
+    ]
+    for copy in xy:
+        copy.start()
+
+    back[...] = dot(tmat[...], dbas[...], 0, 0)
+    rim[0] = back[size : 2 * size, :].astype(bf16)
+    rim[1] = back[2 * size : 3 * size, :].astype(bf16)
+    rim_up = remote(rim.at[0], rim.at[3], rim_s.at[0], rim_r.at[0], (lat - 1, dp))
+    rim_down = remote(rim.at[1], rim.at[2], rim_s.at[1], rim_r.at[1], (lat + 1, dp))
+
+    @pl.when(lat > 0)
+    def _():
+        rim_up.start()
+
+    @pl.when(lat < last)
+    def _():
+        rim_down.start()
+
+    for copy in xy:
+        copy.wait_recv()
+    own = gt.at[y, lat]
+    for n in range(4):
+        s1[n] = (
+            own[n].astype(f32) + r1[0, n].astype(f32) + (r1[1, n].astype(f32) + r1[2, n].astype(f32))
+        ).astype(bf16)
+    zs = [
+        remote(s1.at[(z + o) % 4], r2.at[o - 1], z_s.at[o - 1], z_r.at[o - 1], (lat, z_dps[o - 1]))
+        for o in (1, 2, 3)
+    ]
+    for copy in zs:
+        copy.start()
+
+    @pl.when(lat < last)
+    def _():
+        rim_up.wait_recv()
+
+    @pl.when(lat > 0)
+    def _():
+        rim_down.wait_recv()
+
+    gin_ref[0, 0] = (
+        cot[...].astype(f32) + back[0:size, :] + rim[2].astype(f32) + rim[3].astype(f32)
+    ).astype(bf16)
+
+    for copy in zs:
+        copy.wait_recv()
+    q[lat] = (
+        s1[z].astype(f32) + r2[0].astype(f32) + (r2[1].astype(f32) + r2[2].astype(f32))
+    ).astype(bf16)
+    lats = [
+        remote(q.at[lat], q.at[lat], lat_s.at[n], lat_r.at[n], (other, dp))
+        for n, other in enumerate((x_lat, c_lat, xc_lat))
+    ]
+    arrive = [
+        remote(q.at[other], q.at[other], lat_s.at[n], lat_r.at[n], (other, dp))
+        for n, other in enumerate((x_lat, c_lat, xc_lat))
+    ]
+    for n in (2, 0, 1):
+        lats[n].start()
+    rr = lax.broadcasted_iota(jnp.int32, (144, 144), 0)
+    cc = lax.broadcasted_iota(jnp.int32, (144, 144), 1)
+    kc = (cc >= 48).astype(jnp.int32) + (cc >= 96).astype(jnp.int32)
+    order = jnp.where(rr == 3 * (cc - 48 * kc) + kc, 1.0, 0.0).astype(bf16)
+    factor = jnp.exp2(-scale_ref[...].astype(f32)) * (1.0 / math.sqrt(4 * 8 * size))
+    for copy in arrive:
+        copy.wait_recv()
+    for t in range(27):
+        part, at = divmod(t, 7)
+        g, j = divmod(t, 3)
+        gk[g * TILE : (g + 1) * TILE, j * LANES : (j + 1) * LANES] = q[part, at * TILE : (at + 1) * TILE, :]
+    grad = dot(order, gk[...], 1, 0)
+    for j in range(3):
+        wg_ref[:, j * LANES : (j + 1) * LANES] = grad[:, j * LANES : (j + 1) * LANES] * factor[:, j : j + 1]
+
+    @pl.when(lat < last)
+    def _():
+        down.wait_send()
+        rim_down.wait_send()
+
+    @pl.when(lat > 0)
+    def _():
+        up.wait_send()
+        rim_up.wait_send()
+
+    for copy in [send_bas, send_dmix] + xy + zs + lats:
+        copy.wait_send()
+
+
+def local_fused(inputs, cotangent, kernel_tiles, mix_weight, slot_row, slot_lon, slot_count, scale_exps):
+    size, chans = inputs.shape[2], inputs.shape[3]
+    basis = kernel_tiles.shape[2]
+    bf16, f32 = jnp.bfloat16, jnp.float32
+    dma = pltpu.SemaphoreType.DMA
+    vmem = pl.BlockSpec(memory_space=pltpu.VMEM)
+    smem = pl.BlockSpec(memory_space=pltpu.SMEM)
+    hbm = pl.BlockSpec(memory_space=pl.ANY)
+    return pl.pallas_call(
+        fused,
+        out_shape=(
+            jax.ShapeDtypeStruct(inputs.shape, bf16),
+            jax.ShapeDtypeStruct(inputs.shape, bf16),
+            jax.ShapeDtypeStruct((basis * chans // 8, chans), f32),
+        ),
+        in_specs=[smem, smem, vmem, hbm, hbm, hbm, hbm],
+        out_specs=(vmem, vmem, vmem),
+        scratch_shapes=[
+            pltpu.VMEM((3, size, chans), bf16),
+            pltpu.VMEM((size, chans), bf16),
+            pltpu.VMEM(kernel_tiles.shape[1:], bf16),
+            pltpu.VMEM(mix_weight.shape, bf16),
+            pltpu.VMEM((basis, chans, chans), bf16),
+            pltpu.VMEM((basis * size, 3 * size), bf16),
+            pltpu.VMEM((2, basis * size, chans), bf16),
+            pltpu.VMEM((2, size, chans), bf16),
+            pltpu.VMEM((basis * size, chans), bf16),
+            pltpu.VMEM((3 * size, chans), f32),
+            pltpu.VMEM((4, size, chans), bf16),
+            pltpu.VMEM((2, 4, 4, 7 * TILE, LANES), bf16),
+            pltpu.VMEM((3, 4, 7 * TILE, LANES), bf16),
+            pltpu.VMEM((4, 7 * TILE, LANES), bf16),
+            pltpu.VMEM((3, 7 * TILE, LANES), bf16),
+            pltpu.VMEM((4, 7 * TILE, LANES), bf16),
+            pltpu.VMEM((144, chans), bf16),
+            dma((4,)), dma((2,)), dma((2,)), dma((2,)), dma((2,)), dma((3,)), dma((3,)),
+            dma((2,)), dma((2,)), dma((3,)), dma((3,)), dma((3,)), dma((3,)),
+        ],
+        compiler_params=pltpu.CompilerParams(
+            collective_id=0, has_side_effects=True, vmem_limit_bytes=40 * 1024 * 1024
+        ),
+        cost_estimate=pl.CostEstimate(flops=10**9, bytes_accessed=3 * 10**6, transcendentals=50000),
+    )(slot_row, slot_count, scale_exps, inputs, cotangent, kernel_tiles, mix_weight)
+
+
+def fits(mesh):
+    return mesh.shape["lat"] == 4 and mesh.shape["dp"] == 8
+
+
 def solution(mesh):
     in_specs = (
         P("dp", "lat", None, None),
@@ -108,4 +395,5 @@
         P("dp", None),
     )
     out_specs = (P("dp", "lat", None, None), P("dp", "lat", None, None), P("dp", None))
-    return jax.shard_map(local, mesh=mesh, in_specs=in_specs, out_specs=out_specs, check_vma=False)
+    body = local_fused if fits(mesh) else local
+    return jax.shard_map(body, mesh=mesh, in_specs=in_specs, out_specs=out_specs, check_vma=False)

time: 144 us -> 34.7 us (0.24)
  waiting for transfers between devices: 86 us -> 0 us
  Pallas kernels: 0 us -> 26.3 us
  between operations: 22.7 us -> 1.32 us
  starting transfers between devices: 10.8 us -> 0 us
  matrix products: 8.56 us -> 0 us
  other arithmetic: 5.63 us -> 0 us
  local copies, waits for them, and re-layouts: 9.43 us -> 6.77 us
    reduce_scatter x1 -> x0, waiting for transfers between devices: 53.7 us -> none  [local(): lax.psum_scatter(partial_value, 'dp', scatter_dimension=0, tiled=True)]
    psum x1 -> x0, waiting for transfers between devices: 32.3 us -> none  [local(): grad_total = lax.psum(row_part, 'lat')]
    pallas_call x0 -> x1, Pallas kernels: none -> 26.3 us  [local_fused(): pl.pallas_call(fused, out_shape=(jax.ShapeDtypeStruct(inputs.shape, bf16)...]
    ppermute x4 -> x0, starting transfers between devices: 10.7 us -> none  [the longest x2 8.13 us: extended_2(): lax.ppermute(tail, axis, [(i, (i + 1) % count) for i in range(ends)])]
    dot_general x15 -> x0, matrix products: 8.56 us -> none  [the longest x6 5.43 us: local(): jnp.einsum('rkpq,rjpkc->rjqc', masked[slot_index], dbasis, preferred_elem...]
    unnamed x16 -> x14, local copies, waits for them, and re-layouts: 1.4 us -> 6.77 us
    reshape x2 -> x0, local copies, waits for them, and re-layouts: 4.53 us -> none  [the longest x1 2.28 us: local(): partial_value = major_part.reshape(basis_count, channels, channels).trans...]
    another operation x4 -> x0, other arithmetic: 2.31 us -> none
  transfers between devices with their start and end apart: 6 -> 0, of which waited for: 2 -> 0; matrix products, arithmetic and copies ran while one was open for 10% -> 0% of each run, Pallas kernels for 0% -> 0%
where the time goes in v1:
time: 34.7 us; the launch traced here: 34.4 us
  Pallas kernels  26.3 us (76%)
  local copies, waits for them, and re-layouts  6.77 us (20%)
  between operations  1.32 us (4%)
    pallas_call x1, Pallas kernels, local_fused(): pl.pallas_call(fused, out_shape=(jax.ShapeDtypeStruct(inputs.shape, bf16)...  26.3 us
    unnamed x14, local copies, waits for them, and re-layouts  6.77 us

profile of v1, /device:TPU:0, one launch (start us, length us, event | category | flops | bytes accessed | tf_op | source)
XLA Modules:
  0.0 34.4 jit_solution(3866786079769053206)
XLA Ops:
  1.3 0.0 copy-start.4
  1.3 0.8 %copy.10.scale_ref = s32[144,3]{1,0:T(8,128)S(1)} copy(s32[144,3]{0,1:T(4,128)} %param.14) | data formatting | bytes 3456 | tf_op args[7]
  2.1 0.0 copy-done.4
  2.1 0.0 copy-start
  2.1 1.2 %copy-done = bf16[1152,384]{1,0:T(8,128)(2,1)S(1)} copy-done((bf16[1152,384]{1,0:T(8,128)(2,1)S(1)}, bf16[1152,384]{1,0:T(8,128)(2,1)}, u32[]{:S(2)}) %copy-start) | copy-done | bytes 884760
  3.3 0.0 copy-start.1
  3.3 1.1 %copy-done.1 = bf16[1,6,3,128,128]{4,3,2,1,0:T(8,128)(2,1)S(1)} copy-done((bf16[1,6,3,128,128]{4,3,2,1,0:T(8,128)(2,1)S(1)}, bf16[1,6,3,128,128]{4,3,2,1,0:T(8,128)(2,1)}, u32[]{:S(2)}) %copy-start.1) | copy-done | bytes 589848
  4.3 0.0 copy-start.2
  4.3 0.9 %copy-done.2 = bf16[1,1,128,384]{3,2,1,0:T(8,128)(2,1)S(1)} copy-done((bf16[1,1,128,384]{3,2,1,0:T(8,128)(2,1)S(1)}, bf16[1,1,128,384]{3,2,1,0:T(8,128)(2,1)}, u32[]{:S(2)}) %copy-start.2) | copy-done | bytes 98328
  5.2 0.0 copy-start.3
  5.2 0.9 %copy-done.3 = bf16[1,1,128,384]{3,2,1,0:T(8,128)(2,1)S(1)} copy-done((bf16[1,1,128,384]{3,2,1,0:T(8,128)(2,1)S(1)}, bf16[1,1,128,384]{3,2,1,0:T(8,128)(2,1)}, u32[]{:S(2)}) %copy-start.3) | copy-done | bytes 98328
  6.1 26.3 %shard_map.94 = (bf16[1,1,128,384]{3,2,1,0:T(8,128)(2,1)S(1)}, bf16[1,1,128,384]{3,2,1,0:T(8,128)(2,1)S(1)}, f32[144,384]{1,0:T(8,128)S(1)}) custom-call(s32[1,6]{1,0:T(1,128)S(1)} %copy-done.4, s32[1]{0:T(128)S(6)} %copy.14.count_ref, s32[144,3]{1,0:T(8,128)S(1)} %copy.10.scale_ref, bf16[1,1,128,384]{3,2,1,0:T(8,128)(2,1)S(1)} %copy-done.2, ...), custom_call_target="tpu_custom_call" | custom-call | flops 1000000000 | bytes 3000000 | tf_op jit(solution)/shard_map/pallas_call | solution.py:345
  32.5 0.6 %copy.15 = bf16[1,1,128,384]{3,2,1,0:T(8,128)(2,1)} copy(bf16[1,1,128,384]{3,2,1,0:T(8,128)(2,1)S(1)} %get-tuple-element.6) | data formatting | bytes 196608
  33.1 0.6 %copy.16 = bf16[1,1,128,384]{3,2,1,0:T(8,128)(2,1)} copy(bf16[1,1,128,384]{3,2,1,0:T(8,128)(2,1)S(1)} %get-tuple-element.7) | data formatting | bytes 196608
  33.8 0.7 %copy.17 = f32[144,384]{1,0:T(8,128)} copy(f32[144,384]{1,0:T(8,128)S(1)} %get-tuple-element.8) | data formatting | bytes 442368
Async XLA Ops:
  1.3 0.8 %copy-start.4 = (s32[1,6]{1,0:T(1,128)S(1)}, s32[1,6]{1,0:T(1,128)}, u32[]{:S(2)}) copy-start(s32[1,6]{1,0:T(1,128)} %row_ref.1) | copy-start | bytes 76
  2.1 1.2 %copy-start = (bf16[1152,384]{1,0:T(8,128)(2,1)S(1)}, bf16[1152,384]{1,0:T(8,128)(2,1)}, u32[]{:S(2)}) copy-start(bf16[1152,384]{1,0:T(8,128)(2,1)} %w_hbm.1) | copy-start | bytes 2654212
  3.3 1.1 %copy-start.1 = (bf16[1,6,3,128,128]{4,3,2,1,0:T(8,128)(2,1)S(1)}, bf16[1,6,3,128,128]{4,3,2,1,0:T(8,128)(2,1)}, u32[]{:S(2)}) copy-start(bf16[1,6,3,128,128]{4,3,2,1,0:T(8,128)(2,1)} %tiles_hbm.1) | copy-start | bytes 1769476
  4.3 0.9 %copy-start.2 = (bf16[1,1,128,384]{3,2,1,0:T(8,128)(2,1)S(1)}, bf16[1,1,128,384]{3,2,1,0:T(8,128)(2,1)}, u32[]{:S(2)}) copy-start(bf16[1,1,128,384]{3,2,1,0:T(8,128)(2,1)} %x_hbm.1) | copy-start | bytes 294916
  5.2 0.9 %copy-start.3 = (bf16[1,1,128,384]{3,2,1,0:T(8,128)(2,1)S(1)}, bf16[1,1,128,384]{3,2,1,0:T(8,128)(2,1)}, u32[]{:S(2)}) copy-start(bf16[1,1,128,384]{3,2,1,0:T(8,128)(2,1)} %cot_hbm.1) | copy-start | bytes 294916

commit v2 on v1

--- a/solution.py
+++ b/solution.py
@@ -101,6 +101,7 @@
 MESH = pl.DeviceIdType.MESH
 TILE = 16
 LANES = 128
+CHUNKS = (4, 3)
 
 
 def dot(a, b, da, db):
@@ -110,7 +111,7 @@
 def fused(
     row_ref, count_ref, scale_ref, x_hbm, cot_hbm, tiles_hbm, w_hbm,
     out_ref, gin_ref, wg_ref,
-    xs, cot, tiles, w, wk, tmat, bas, dmix, dbas, back, rim, gt, r1, s1, r2, q, gk,
+    xs, cot, tiles, w, wk, tmat, bas, dmix, dbas, back, rim, gt_a, gt_b, r1_a, r1_b, s1_a, s1_b, r2_a, r2_b, q_a, q_b, gk,
     load_sem, halo_s, halo_r, fac_s, fac_r, xy_s, xy_r, rim_s, rim_r, z_s, z_r, lat_s, lat_r,
 ):
     lat = lax.axis_index("lat")
@@ -172,7 +173,8 @@
         xs[2] = jnp.zeros(xs.shape[1:], bf16)
         rim[3] = jnp.zeros(rim.shape[1:], bf16)
 
-    gt[:, 3, :, 96:112, :] = jnp.zeros((2, 4, TILE, LANES), bf16)
+    gts, r1s, s1s, r2s, qs = (gt_a, gt_b), (r1_a, r1_b), (s1_a, s1_b), (r2_a, r2_b), (q_a, q_b)
+    gt_b[:, 3, :, 32:48, :] = jnp.zeros((2, 4, TILE, LANES), bf16)
 
     loads[0].wait()
     count = count_ref[0]
@@ -230,25 +232,35 @@
     send_bas.wait_recv()
     send_dmix.wait_recv()
     both = dmix[...].reshape(2 * size, chans)
+
+    def exchange(h):
+        gt, r1 = gts[h], r1s[h]
+        ends = (
+            (2, gt.at[1 - y, x_lat], (x_lat, y_dp)),
+            (0, gt.at[y, x_lat], (x_lat, dp)),
+            (1, gt.at[1 - y, lat], (lat, y_dp)),
+        )
+        copies = [remote(src, r1.at[n], xy_s.at[3 * h + n], xy_r.at[3 * h + n], to) for n, src, to in ends]
+        for copy in copies:
+            copy.start()
+        return copies
+
+    xy = [None, None]
     for k in range(basis):
         lhs = jnp.concatenate([bas[0, k * size : (k + 1) * size, :], bas[1, k * size : (k + 1) * size, :]], axis=0)
         grad = dot(lhs, both, 0, 0).astype(bf16)
         for d in range(8):
             for i in range(3):
                 for j in range(3):
-                    part, at = divmod((k * 3 + i) * 3 + j, 7)
+                    at, part = divmod((k * 3 + i) * 3 + j, 4)
+                    h, at = (0, at) if at < CHUNKS[0] else (1, at - CHUNKS[0])
                     lo = 48 * d + TILE * i
-                    gt[d % 2, part, d // 2, at * TILE : (at + 1) * TILE, :] = grad[
+                    gts[h][d % 2, part, d // 2, at * TILE : (at + 1) * TILE, :] = grad[
                         lo : lo + TILE, j * LANES : (j + 1) * LANES
                     ]
-
-    xy = [
-        remote(gt.at[1 - y, x_lat], r1.at[2], xy_s.at[2], xy_r.at[2], (x_lat, y_dp)),
-        remote(gt.at[y, x_lat], r1.at[0], xy_s.at[0], xy_r.at[0], (x_lat, dp)),
-        remote(gt.at[1 - y, lat], r1.at[1], xy_s.at[1], xy_r.at[1], (lat, y_dp)),
-    ]
-    for copy in xy:
-        copy.start()
+        if k == 1:
+            xy[0] = exchange(0)
+    xy[1] = exchange(1)
 
     back[...] = dot(tmat[...], dbas[...], 0, 0)
     rim[0] = back[size : 2 * size, :].astype(bf16)
@@ -264,19 +276,26 @@
     def _():
         rim_down.start()
 
-    for copy in xy:
-        copy.wait_recv()
-    own = gt.at[y, lat]
-    for n in range(4):
-        s1[n] = (
-            own[n].astype(f32) + r1[0, n].astype(f32) + (r1[1, n].astype(f32) + r1[2, n].astype(f32))
-        ).astype(bf16)
-    zs = [
-        remote(s1.at[(z + o) % 4], r2.at[o - 1], z_s.at[o - 1], z_r.at[o - 1], (lat, z_dps[o - 1]))
-        for o in (1, 2, 3)
-    ]
-    for copy in zs:
-        copy.start()
+    zs = []
+    for h in range(2):
+        for copy in xy[h]:
+            copy.wait_recv()
+        own, r1, s1, r2 = gts[h].at[y, lat], r1s[h], s1s[h], r2s[h]
+        for n in range(4):
+            s1[n] = (
+                own[n].astype(f32) + r1[0, n].astype(f32) + (r1[1, n].astype(f32) + r1[2, n].astype(f32))
+            ).astype(bf16)
+        zs.append(
+            [
+                remote(
+                    s1.at[(z + o) % 4], r2.at[o - 1], z_s.at[3 * h + o - 1], z_r.at[3 * h + o - 1],
+                    (lat, z_dps[o - 1]),
+                )
+                for o in (2, 1, 3)
+            ]
+        )
+        for copy in zs[h]:
+            copy.start()
 
     @pl.when(lat < last)
     def _():
@@ -290,35 +309,38 @@
         cot[...].astype(f32) + back[0:size, :] + rim[2].astype(f32) + rim[3].astype(f32)
     ).astype(bf16)
 
-    for copy in zs:
-        copy.wait_recv()
-    q[lat] = (
-        s1[z].astype(f32) + r2[0].astype(f32) + (r2[1].astype(f32) + r2[2].astype(f32))
-    ).astype(bf16)
-    lats = [
-        remote(q.at[lat], q.at[lat], lat_s.at[n], lat_r.at[n], (other, dp))
-        for n, other in enumerate((x_lat, c_lat, xc_lat))
-    ]
-    arrive = [
-        remote(q.at[other], q.at[other], lat_s.at[n], lat_r.at[n], (other, dp))
-        for n, other in enumerate((x_lat, c_lat, xc_lat))
-    ]
-    for n in (2, 0, 1):
-        lats[n].start()
+    lats, arrive = [], []
+    for h in range(2):
+        for copy in zs[h]:
+            copy.wait_recv()
+        s1, r2, q = s1s[h], r2s[h], qs[h]
+        q[lat] = (
+            s1[z].astype(f32) + r2[0].astype(f32) + (r2[1].astype(f32) + r2[2].astype(f32))
+        ).astype(bf16)
+        for n, other in ((2, xc_lat), (0, x_lat), (1, c_lat)):
+            copy = remote(q.at[lat], q.at[lat], lat_s.at[3 * h + n], lat_r.at[3 * h + n], (other, dp))
+            copy.start()
+            lats.append(copy)
+            arrive.append(
+                remote(q.at[other], q.at[other], lat_s.at[3 * h + n], lat_r.at[3 * h + n], (other, dp))
+            )
     rr = lax.broadcasted_iota(jnp.int32, (144, 144), 0)
     cc = lax.broadcasted_iota(jnp.int32, (144, 144), 1)
     kc = (cc >= 48).astype(jnp.int32) + (cc >= 96).astype(jnp.int32)
     order = jnp.where(rr == 3 * (cc - 48 * kc) + kc, 1.0, 0.0).astype(bf16)
     factor = jnp.exp2(-scale_ref[...].astype(f32)) * (1.0 / math.sqrt(4 * 8 * size))
+    jr = lax.broadcasted_iota(jnp.int32, (3, chans), 0)
+    jc = lax.broadcasted_iota(jnp.int32, (3, chans), 1)
+    spread = jnp.where(jnp.logical_and(jc >= jr * LANES, jc < (jr + 1) * LANES), 1.0, 0.0).astype(f32)
+    factor = dot(factor, spread, 0, 0)
     for copy in arrive:
         copy.wait_recv()
     for t in range(27):
-        part, at = divmod(t, 7)
+        at, part = divmod(t, 4)
+        q, at = (q_a, at) if at < CHUNKS[0] else (q_b, at - CHUNKS[0])
         g, j = divmod(t, 3)
         gk[g * TILE : (g + 1) * TILE, j * LANES : (j + 1) * LANES] = q[part, at * TILE : (at + 1) * TILE, :]
-    grad = dot(order, gk[...], 1, 0)
-    for j in range(3):
-        wg_ref[:, j * LANES : (j + 1) * LANES] = grad[:, j * LANES : (j + 1) * LANES] * factor[:, j : j + 1]
+    wg_ref[...] = dot(order, gk[...], 1, 0) * factor
 
     @pl.when(lat < last)
     def _():
@@ -330,7 +352,7 @@
         up.wait_send()
         rim_up.wait_send()
 
-    for copy in [send_bas, send_dmix] + xy + zs + lats:
+    for copy in [send_bas, send_dmix] + xy[0] + xy[1] + zs[0] + zs[1] + lats:
         copy.wait_send()
 
 
@@ -341,7 +363,7 @@
     dma = pltpu.SemaphoreType.DMA
     vmem = pl.BlockSpec(memory_space=pltpu.VMEM)
     smem = pl.BlockSpec(memory_space=pltpu.SMEM)
-    hbm = pl.BlockSpec(memory_space=pl.ANY)
+    hbm = pl.BlockSpec(memory_space=pltpu.HBM)
     return pl.pallas_call(
         fused,
         out_shape=(
@@ -363,20 +385,20 @@
             pltpu.VMEM((basis * size, chans), bf16),
             pltpu.VMEM((3 * size, chans), f32),
             pltpu.VMEM((4, size, chans), bf16),
-            pltpu.VMEM((2, 4, 4, 7 * TILE, LANES), bf16),
-            pltpu.VMEM((3, 4, 7 * TILE, LANES), bf16),
-            pltpu.VMEM((4, 7 * TILE, LANES), bf16),
-            pltpu.VMEM((3, 7 * TILE, LANES), bf16),
-            pltpu.VMEM((4, 7 * TILE, LANES), bf16),
+            *[pltpu.VMEM((2, 4, 4, n * TILE, LANES), bf16) for n in CHUNKS],
+            *[pltpu.VMEM((3, 4, n * TILE, LANES), bf16) for n in CHUNKS],
+            *[pltpu.VMEM((4, n * TILE, LANES), bf16) for n in CHUNKS],
+            *[pltpu.VMEM((3, n * TILE, LANES), bf16) for n in CHUNKS],
+            *[pltpu.VMEM((4, n * TILE, LANES), bf16) for n in CHUNKS],
             pltpu.VMEM((144, chans), bf16),
-            dma((4,)), dma((2,)), dma((2,)), dma((2,)), dma((2,)), dma((3,)), dma((3,)),
-            dma((2,)), dma((2,)), dma((3,)), dma((3,)), dma((3,)), dma((3,)),
+            dma((4,)), dma((2,)), dma((2,)), dma((2,)), dma((2,)), dma((6,)), dma((6,)),
+            dma((2,)), dma((2,)), dma((6,)), dma((6,)), dma((6,)), dma((6,)),
         ],
         compiler_params=pltpu.CompilerParams(
-            collective_id=0, has_side_effects=True, vmem_limit_bytes=40 * 1024 * 1024
+            collective_id=0, has_side_effects=True, vmem_limit_bytes=65472 * 1024
         ),
         cost_estimate=pl.CostEstimate(flops=10**9, bytes_accessed=3 * 10**6, transcendentals=50000),
-    )(slot_row, slot_count, scale_exps, inputs, cotangent, kernel_tiles, mix_weight)
+    )(slot_row, slot_count, scale_exps.T, inputs, cotangent, kernel_tiles, mix_weight)
 
 
 def fits(mesh):

time: 34.7 us -> 32.4 us (0.934)
  local copies, waits for them, and re-layouts: 6.77 us -> 3.82 us
  Pallas kernels: 26.3 us -> 27.1 us
    unnamed x14 -> x5, local copies, waits for them, and re-layouts: 6.77 us -> 3.82 us
    pallas_call x1, Pallas kernels: 26.3 us -> 27.1 us  [local_fused(): pl.pallas_call(fused, out_shape=(jax.ShapeDtypeStruct(inputs.shape, bf16)...]
where the time goes in v2:
time: 32.4 us; the launch traced here: 32.2 us
  Pallas kernels  27.1 us (84%)
  local copies, waits for them, and re-layouts  3.82 us (12%)
  between operations  1.3 us (4%)
    pallas_call x1, Pallas kernels, local_fused(): pl.pallas_call(fused, out_shape=(jax.ShapeDtypeStruct(inputs.shape, bf16)...  27.1 us
    unnamed x5, local copies, waits for them, and re-layouts  3.82 us

profile of v2, /device:TPU:0, one launch (start us, length us, event | category | flops | bytes accessed | tf_op | source)
XLA Modules:
  0.0 32.2 jit_solution(5018414095213867184)
XLA Ops:
  1.3 27.1 %shard_map.94 = (bf16[1,1,128,384]{3,2,1,0:T(8,128)(2,1)}, bf16[1,1,128,384]{3,2,1,0:T(8,128)(2,1)}, f32[144,384]{1,0:T(8,128)}) custom-call(s32[1,6]{1,0:T(1,128)} %row_ref.1, s32[1]{0:T(128)S(6)} %copy.13.count_ref, s32[3,144]{1,0:T(4,128)} %bitcast.1, bf16[1,1,128,384]{3,2,1,0:T(8,128)(2,1)} %x_hbm.1, bf16[1,1,128,384]{3,2,1,0:T(8,128)(2,1)} %cot_hbm.1, ...), custom_call_target="tpu_custom_call" | custom-call | flops 1000000000 | bytes 3000000 | tf_op jit(solution)/shard_map/pallas_call | solution.py:367
  28.3 0.0 copy-start
  28.4 1.6 %copy.14 = bf16[1,1,128,384]{3,2,1,0:T(8,128)(2,1)} copy(bf16[1,1,128,384]{3,2,1,0:T(8,128)(2,1)} %get-tuple-element.6) | data formatting | bytes 196608
  29.9 1.5 %copy.15 = bf16[1,1,128,384]{3,2,1,0:T(8,128)(2,1)} copy(bf16[1,1,128,384]{3,2,1,0:T(8,128)(2,1)} %get-tuple-element.7) | data formatting | bytes 196608
  31.5 0.0 copy-done
  31.5 0.7 %copy.16 = f32[144,384]{1,0:T(8,128)} copy(f32[144,384]{1,0:T(8,128)S(1)} %copy-done) | data formatting | bytes 442368
Async XLA Ops:
  28.3 3.1 %copy-start = (f32[144,384]{1,0:T(8,128)S(1)}, f32[144,384]{1,0:T(8,128)}, u32[]{:S(2)}) copy-start(f32[144,384]{1,0:T(8,128)} %get-tuple-element.8) | copy-start | bytes 663556

commit v3 on v2

--- a/solution.py
+++ b/solution.py
@@ -356,6 +356,15 @@
         copy.wait_send()
 
 
+def deliver(a_ref, b_ref, c_ref, a_out, b_out, c_out, sems):
+    pairs = ((a_ref, a_out), (b_ref, b_out), (c_ref, c_out))
+    copies = [pltpu.make_async_copy(src, dst, sems.at[n]) for n, (src, dst) in enumerate(pairs)]
+    for copy in copies:
+        copy.start()
+    for copy in copies:
+        copy.wait()
+
+
 def local_fused(inputs, cotangent, kernel_tiles, mix_weight, slot_row, slot_lon, slot_count, scale_exps):
     size, chans = inputs.shape[2], inputs.shape[3]
     basis = kernel_tiles.shape[2]
@@ -364,12 +373,12 @@
     vmem = pl.BlockSpec(memory_space=pltpu.VMEM)
     smem = pl.BlockSpec(memory_space=pltpu.SMEM)
     hbm = pl.BlockSpec(memory_space=pltpu.HBM)
-    return pl.pallas_call(
+    results = pl.pallas_call(
         fused,
         out_shape=(
-            jax.ShapeDtypeStruct(inputs.shape, bf16),
-            jax.ShapeDtypeStruct(inputs.shape, bf16),
-            jax.ShapeDtypeStruct((basis * chans // 8, chans), f32),
+            pltpu.VMEM(inputs.shape, bf16),
+            pltpu.VMEM(inputs.shape, bf16),
+            pltpu.VMEM((basis * chans // 8, chans), f32),
         ),
         in_specs=[smem, smem, vmem, hbm, hbm, hbm, hbm],
         out_specs=(vmem, vmem, vmem),
@@ -395,10 +404,18 @@
             dma((2,)), dma((2,)), dma((6,)), dma((6,)), dma((6,)), dma((6,)),
         ],
         compiler_params=pltpu.CompilerParams(
-            collective_id=0, has_side_effects=True, vmem_limit_bytes=65472 * 1024
+            collective_id=0, has_side_effects=True, vmem_limit_bytes=64960 * 1024
         ),
         cost_estimate=pl.CostEstimate(flops=10**9, bytes_accessed=3 * 10**6, transcendentals=50000),
     )(slot_row, slot_count, scale_exps.T, inputs, cotangent, kernel_tiles, mix_weight)
+    return pl.pallas_call(
+        deliver,
+        out_shape=tuple(jax.ShapeDtypeStruct(one.shape, one.dtype) for one in results),
+        in_specs=[pl.BlockSpec(memory_space=pl.ANY)] * 3,
+        compiler_params=pltpu.CompilerParams(vmem_limit_bytes=32 * 1024 * 1024),
+        out_specs=(hbm,) * 3,
+        scratch_shapes=[dma((3,))],
+    )(*results)
 
 
 def fits(mesh):

time: 32.4 us -> 28.6 us (0.88)
  local copies, waits for them, and re-layouts: 3.82 us -> 0 us
    unnamed x5 -> x0, local copies, waits for them, and re-layouts: 3.82 us -> none
    pallas_call x1 -> x2, Pallas kernels: 27.1 us -> 27.1 us  [the longest x1 26.3 us: local_fused(): pl.pallas_call(fused, out_shape=(pltpu.VMEM(inputs.shape, bf16), pltpu.VM...]
where the time goes in v3:
time: 28.6 us; the launch traced here: 28.4 us
  Pallas kernels  27.1 us (95%)
  between operations  1.29 us (5%)
    pallas_call x1, Pallas kernels, local_fused(): pl.pallas_call(fused, out_shape=(pltpu.VMEM(inputs.shape, bf16), pltpu.VM...  26.3 us
    pallas_call x1, Pallas kernels, local_fused(): pl.pallas_call(deliver, out_shape=tuple((jax.ShapeDtypeStruct(one.shape,...  0.78 us

profile of v3, /device:TPU:0, one launch (start us, length us, event | category | flops | bytes accessed | tf_op | source)
XLA Modules:
  0.0 28.4 jit_solution(5576887003601517700)
XLA Ops:
  1.3 26.3 %shard_map.94 = (bf16[1,1,128,384]{3,2,1,0:T(8,128)(2,1)S(1)}, bf16[1,1,128,384]{3,2,1,0:T(8,128)(2,1)S(1)}, f32[144,384]{1,0:T(8,128)S(1)}) custom-call(s32[1,6]{1,0:T(1,128)} %row_ref.1, s32[1]{0:T(128)S(6)} %copy.10.count_ref, s32[3,144]{1,0:T(4,128)} %bitcast.1, bf16[1,1,128,384]{3,2,1,0:T(8,128)(2,1)} %x_hbm.1, bf16[1,1,128,384]{3,2,1,0:T(8,128)(2,1)} %cot_hbm.1, ...), custom_call_target="tpu_custom_call" | custom-call | flops 1000000000 | bytes 3000000 | tf_op jit(solution)/shard_map/pallas_call | solution.py:376
  27.6 0.8 %shard_map.95 = (bf16[1,1,128,384]{3,2,1,0:T(8,128)(2,1)}, bf16[1,1,128,384]{3,2,1,0:T(8,128)(2,1)}, f32[144,384]{1,0:T(8,128)}) custom-call(bf16[1,1,128,384]{3,2,1,0:T(8,128)(2,1)S(1)} %get-tuple-element.6.a_ref, bf16[1,1,128,384]{3,2,1,0:T(8,128)(2,1)S(1)} %get-tuple-element.7.b_ref, f32[144,384]{1,0:T(8,128)S(1)} %get-tuple-element.8.c_ref), custom_call_target="tpu_custom_call" | custom-call | tf_op jit(solution)/shard_map/pallas_call | solution.py:411

commit v4 on v3

--- a/solution.py
+++ b/solution.py
@@ -268,46 +268,32 @@
     rim_up = remote(rim.at[0], rim.at[3], rim_s.at[0], rim_r.at[0], (lat - 1, dp))
     rim_down = remote(rim.at[1], rim.at[2], rim_s.at[1], rim_r.at[1], (lat + 1, dp))
 
-    @pl.when(lat > 0)
-    def _():
-        rim_up.start()
-
-    @pl.when(lat < last)
-    def _():
-        rim_down.start()
-
     zs = []
     for h in range(2):
         for copy in xy[h]:
             copy.wait_recv()
         own, r1, s1, r2 = gts[h].at[y, lat], r1s[h], s1s[h], r2s[h]
-        for n in range(4):
+        sends = []
+        for o in (2, 1, 3, 4):
+            n = (z + o) % 4
             s1[n] = (
                 own[n].astype(f32) + r1[0, n].astype(f32) + (r1[1, n].astype(f32) + r1[2, n].astype(f32))
             ).astype(bf16)
-        zs.append(
-            [
-                remote(
-                    s1.at[(z + o) % 4], r2.at[o - 1], z_s.at[3 * h + o - 1], z_r.at[3 * h + o - 1],
-                    (lat, z_dps[o - 1]),
+            if o < 4:
+                copy = remote(
+                    s1.at[n], r2.at[o - 1], z_s.at[3 * h + o - 1], z_r.at[3 * h + o - 1], (lat, z_dps[o - 1])
                 )
-                for o in (2, 1, 3)
-            ]
-        )
-        for copy in zs[h]:
-            copy.start()
+                copy.start()
+                sends.append(copy)
+        zs.append(sends)
+
+    @pl.when(lat > 0)
+    def _():
+        rim_up.start()
 
     @pl.when(lat < last)
     def _():
-        rim_up.wait_recv()
-
-    @pl.when(lat > 0)
-    def _():
-        rim_down.wait_recv()
-
-    gin_ref[0, 0] = (
-        cot[...].astype(f32) + back[0:size, :] + rim[2].astype(f32) + rim[3].astype(f32)
-    ).astype(bf16)
+        rim_down.start()
 
     lats, arrive = [], []
     for h in range(2):
@@ -324,6 +310,18 @@
             arrive.append(
                 remote(q.at[other], q.at[other], lat_s.at[3 * h + n], lat_r.at[3 * h + n], (other, dp))
             )
+    @pl.when(lat < last)
+    def _():
+        rim_up.wait_recv()
+
+    @pl.when(lat > 0)
+    def _():
+        rim_down.wait_recv()
+
+    gin_ref[0, 0] = (
+        cot[...].astype(f32) + back[0:size, :] + rim[2].astype(f32) + rim[3].astype(f32)
+    ).astype(bf16)
+
     rr = lax.broadcasted_iota(jnp.int32, (144, 144), 0)
     cc = lax.broadcasted_iota(jnp.int32, (144, 144), 1)
     kc = (cc >= 48).astype(jnp.int32) + (cc >= 96).astype(jnp.int32)

time: 28.6 us -> 27.6 us (0.965)
  Pallas kernels: 27.1 us -> 26.1 us
    pallas_call x1, Pallas kernels: 26.3 us -> 25.3 us  [local_fused(): pl.pallas_call(fused, out_shape=(pltpu.VMEM(inputs.shape, bf16), pltpu.VM...]
where the time goes in v4:
time: 27.6 us; the launch traced here: 27.4 us
  Pallas kernels  26.1 us (95%)
  between operations  1.29 us (5%)
    pallas_call x1, Pallas kernels, local_fused(): pl.pallas_call(fused, out_shape=(pltpu.VMEM(inputs.shape, bf16), pltpu.VM...  25.3 us
    pallas_call x1, Pallas kernels, local_fused(): pl.pallas_call(deliver, out_shape=tuple((jax.ShapeDtypeStruct(one.shape,...  0.78 us

profile of v4, /device:TPU:0, one launch (start us, length us, event | category | flops | bytes accessed | tf_op | source)
XLA Modules:
  0.0 27.4 jit_solution(3459065663623269856)
XLA Ops:
  1.3 25.3 %shard_map.94 = (bf16[1,1,128,384]{3,2,1,0:T(8,128)(2,1)S(1)}, bf16[1,1,128,384]{3,2,1,0:T(8,128)(2,1)S(1)}, f32[144,384]{1,0:T(8,128)S(1)}) custom-call(s32[1,6]{1,0:T(1,128)} %row_ref.1, s32[1]{0:T(128)S(6)} %copy.10.count_ref, s32[3,144]{1,0:T(4,128)} %bitcast.1, bf16[1,1,128,384]{3,2,1,0:T(8,128)(2,1)} %x_hbm.1, bf16[1,1,128,384]{3,2,1,0:T(8,128)(2,1)} %cot_hbm.1, ...), custom_call_target="tpu_custom_call" | custom-call | flops 1000000000 | bytes 3000000 | tf_op jit(solution)/shard_map/pallas_call | solution.py:374
  26.6 0.8 %shard_map.95 = (bf16[1,1,128,384]{3,2,1,0:T(8,128)(2,1)}, bf16[1,1,128,384]{3,2,1,0:T(8,128)(2,1)}, f32[144,384]{1,0:T(8,128)}) custom-call(bf16[1,1,128,384]{3,2,1,0:T(8,128)(2,1)S(1)} %get-tuple-element.6.a_ref, bf16[1,1,128,384]{3,2,1,0:T(8,128)(2,1)S(1)} %get-tuple-element.7.b_ref, f32[144,384]{1,0:T(8,128)S(1)} %get-tuple-element.8.c_ref), custom_call_target="tpu_custom_call" | custom-call | tf_op jit(solution)/shard_map/pallas_call | solution.py:409

commit v5 on v4

--- a/solution.py
+++ b/solution.py
@@ -204,6 +204,7 @@
 
     loads[2].wait()
     loads[3].wait()
+    middle = dot(tmat[:, 0:size], xs[0], 1, 0)
 
     @pl.when(lat > 0)
     def _():
@@ -213,7 +214,7 @@
     def _():
         up.wait_recv()
 
-    bas[0] = dot(tmat[...], xs[...].reshape(3 * size, chans), 1, 0).astype(bf16)
+    bas[0] = (middle + dot(tmat[:, size : 3 * size], xs[1:3].reshape(2 * size, chans), 1, 0)).astype(bf16)
     send_bas = remote(bas.at[0], bas.at[1], fac_s.at[0], fac_r.at[0], (c_lat, dp))
     send_bas.start()
     mixed = dot(bas[0, 0:size, :], wk[0], 1, 0)

time: 27.6 us -> 27.6 us (level)
  no operation moved by 1% of the time
where the time goes in v5:
time: 27.6 us; the launch traced here: 27.4 us
  Pallas kernels  26.1 us (95%)
  between operations  1.29 us (5%)
    pallas_call x1, Pallas kernels, local_fused(): pl.pallas_call(fused, out_shape=(pltpu.VMEM(inputs.shape, bf16), pltpu.VM...  25.3 us
    pallas_call x1, Pallas kernels, local_fused(): pl.pallas_call(deliver, out_shape=tuple((jax.ShapeDtypeStruct(one.shape,...  0.78 us

profile of v5, /device:TPU:0, one launch (start us, length us, event | category | flops | bytes accessed | tf_op | source)
XLA Modules:
  0.0 27.4 jit_solution(18242482714552204271)
XLA Ops:
  1.3 25.3 %shard_map.94 = (bf16[1,1,128,384]{3,2,1,0:T(8,128)(2,1)S(1)}, bf16[1,1,128,384]{3,2,1,0:T(8,128)(2,1)S(1)}, f32[144,384]{1,0:T(8,128)S(1)}) custom-call(s32[1,6]{1,0:T(1,128)} %row_ref.1, s32[1]{0:T(128)S(6)} %copy.10.count_ref, s32[3,144]{1,0:T(4,128)} %bitcast.1, bf16[1,1,128,384]{3,2,1,0:T(8,128)(2,1)} %x_hbm.1, bf16[1,1,128,384]{3,2,1,0:T(8,128)(2,1)} %cot_hbm.1, ...), custom_call_target="tpu_custom_call" | custom-call | flops 1000000000 | bytes 3000000 | tf_op jit(solution)/shard_map/pallas_call | solution.py:375
  26.6 0.8 %shard_map.95 = (bf16[1,1,128,384]{3,2,1,0:T(8,128)(2,1)}, bf16[1,1,128,384]{3,2,1,0:T(8,128)(2,1)}, f32[144,384]{1,0:T(8,128)}) custom-call(bf16[1,1,128,384]{3,2,1,0:T(8,128)(2,1)S(1)} %get-tuple-element.6.a_ref, bf16[1,1,128,384]{3,2,1,0:T(8,128)(2,1)S(1)} %get-tuple-element.7.b_ref, f32[144,384]{1,0:T(8,128)S(1)} %get-tuple-element.8.c_ref), custom_call_target="tpu_custom_call" | custom-call | tf_op jit(solution)/shard_map/pallas_call | solution.py:410
